TPU v7x, 32 devices: a whole 2x2x4 slice. The times are simulated.
32 devices in a mesh: groups: 2 (over y), col: 4 (over z), row: 4 (over x, core).
Axes of the slice: x: 2, y: 2, z: 4, core: 2. Of those that a mesh axis runs over, the one named last changes fastest.
Arguments:
- pair_slab: bfloat16 [128, 512, 128], P(('groups', 'row'), 'col'), parts along dimension 0, may hold values from -6 to 6
- tile_pair: bfloat16 [8, 2, 128, 128, 128], P(('groups', 'col'), None, 'row'), parts along dimension 0, may hold values from -6 to 6
- tile_cotan: bfloat16 [8, 2, 128, 128, 128], P(('groups', 'col'), None, 'row'), parts along dimension 0, may hold values from -6 to 6
- tile_rows: int32 [8, 2], P(('groups', 'col')), parts along dimension 0, may hold values from 0 to 3, as said below
- tile_count: int32 [8], P(('groups', 'col')), parts along dimension 0, may hold values from 1 to 2, as said below
- norm_gain: float32 [128], replicated, may hold values from 0.5 to 1.5
- norm_bias: float32 [128], replicated, may hold values from -2.5 to 2.5
- w_in: bfloat16 [128, 512], replicated, may hold values from -0.5 to 0.5
- out_gain: float32 [128], replicated, may hold values from 0.5 to 1.5
- out_bias: float32 [128], replicated, may hold values from -2.5 to 2.5
- w_out: bfloat16 [128, 128], replicated, may hold values from -0.5 to 0.5
- w_gate: bfloat16 [128, 128], replicated, may hold values from -0.5 to 0.5
Outputs:
- update: bfloat16 [8, 2, 128, 128, 128], P(('groups', 'col'), None, 'row'), parts along dimension 0
- grad_slab: bfloat16 [128, 512, 128], P(('groups', 'row'), 'col'), parts along dimension 0
- grad_tiles: bfloat16 [8, 2, 128, 128, 128], P(('groups', 'col'), None, 'row'), parts along dimension 0
- grad_in_w: float32 [256, 512], P('groups'), parts along dimension 0
- grad_out_w: float32 [256, 128], P('groups'), parts along dimension 0
- grad_gate_w: float32 [256, 128], P('groups'), parts along dimension 0
There are 2 independent parts, one for each index of `groups`. A program takes and returns all parts, laid end to end along the dimension named above; an argument that names none is the same for every part. Nothing has to cross between parts.
Inputs may be any that keep to these rules, and one draw needn't show every extreme that they name: `tile_count`: every column block has at least one active slot and some column block has all 2 active. `tile_rows`: the row blocks named by the slots of one column block are distinct; slots at or past the count are inactive.
All inputs are finite; a program needn't handle non-finite values.
Results may differ from a plain program's by a relative error of at most 0.015.
Values may be sent and summed in bfloat16 or wider, within the bound.
A program may use at most 128 MiB of HBM per device.

v0:
```python
import jax
import jax.numpy as jnp
from jax import lax
from jax.sharding import PartitionSpec as P

epsilon = 1e-05


def normalize(values):
    center = values - jnp.mean(values, axis=-1, keepdims=True)
    variance = jnp.mean(center * center, axis=-1, keepdims=True)
    inverse = lax.rsqrt(variance + epsilon)
    return (center * inverse, inverse)


def norm_back(grad_in, centred, inverse, gain):
    scaled = grad_in * gain
    first = jnp.mean(scaled, axis=-1, keepdims=True)
    second = jnp.mean(scaled * centred, axis=-1, keepdims=True)
    return inverse * (scaled - first - centred * second)


def rounded(values):
    return lax.optimization_barrier(values.astype(jnp.bfloat16)).astype(jnp.float32)


def body(
    pair_slab,
    tile_pair,
    tile_cotan,
    tile_rows,
    tile_count,
    norm_gain,
    norm_bias,
    w_in,
    out_gain,
    out_bias,
    w_out,
    w_gate,
):
    k_local, tile_len, channels = pair_slab.shape
    hidden_w = w_out.shape[0]
    slots = tile_rows.shape[1]
    row_count = lax.axis_size("row")
    col_count = lax.axis_size("col")
    row_part = tile_len // row_count
    slab_hat, slab_inv = normalize(pair_slab.astype(jnp.float32))
    slab_norm = (slab_hat * norm_gain + norm_bias).astype(jnp.bfloat16)
    flat_norm = slab_norm.reshape(-1, channels)
    project = jnp.dot(flat_norm, w_in, preferred_element_type=jnp.float32).reshape(
        k_local, tile_len, 4 * hidden_w
    )
    left_proj = project[..., :hidden_w]
    left_sig = jax.nn.sigmoid(project[..., hidden_w : 2 * hidden_w])
    right_proj = project[..., 2 * hidden_w : 3 * hidden_w]
    right_sig = jax.nn.sigmoid(project[..., 3 * hidden_w :])
    left_edges = (left_sig * left_proj).astype(jnp.bfloat16)
    right_edges = (right_sig * right_proj).astype(jnp.bfloat16)
    row_blocks = tile_rows[0]
    active = (jnp.arange(slots) < tile_count[0]).astype(jnp.float32)
    selector = (row_blocks[:, None] == jnp.arange(col_count)[None, :]).astype(jnp.float32) * active[
        :, None
    ]
    spread = lax.all_to_all(
        left_edges.reshape(k_local, row_count, row_part, hidden_w),
        "row",
        split_axis=1,
        concat_axis=0,
        tiled=True,
    )
    panels = lax.all_gather(spread, "col", axis=1, tiled=True)
    chosen = jnp.take(panels, row_blocks, axis=1)
    right_full = lax.all_gather(right_edges, "row", axis=0, tiled=True)
    grouped = jnp.einsum(
        "gksih,gkjh->gsijh",
        chosen.reshape(row_count, k_local, slots, row_part, hidden_w),
        right_full.reshape(row_count, k_local, tile_len, hidden_w),
        preferred_element_type=jnp.float32,
    )
    combined = jnp.sum(rounded(grouped), axis=0)
    comb_hat, comb_inv = normalize(combined)
    comb_norm = (comb_hat * out_gain + out_bias).astype(jnp.bfloat16)
    pair_hat, pair_inv = normalize(tile_pair[0].astype(jnp.float32))
    pair_norm = (pair_hat * norm_gain + norm_bias).astype(jnp.bfloat16)
    flat_comb = comb_norm.reshape(-1, hidden_w)
    flat_pair = pair_norm.reshape(-1, channels)
    mixed = jnp.dot(flat_comb, w_out, preferred_element_type=jnp.float32)
    gate = jax.nn.sigmoid(jnp.dot(flat_pair, w_gate, preferred_element_type=jnp.float32))
    row_mask = jnp.repeat(active, row_part * tile_len)[:, None]
    update = (row_mask * gate * mixed).astype(jnp.bfloat16)
    cotan = tile_cotan[0].astype(jnp.float32).reshape(-1, channels) * row_mask
    grad_mixed = (cotan * gate).astype(jnp.bfloat16)
    grad_logit = (cotan * mixed * gate * (1.0 - gate)).astype(jnp.bfloat16)
    grad_out_w = jnp.dot(flat_comb.T, grad_mixed, preferred_element_type=jnp.float32)
    grad_gate_w = jnp.dot(flat_pair.T, grad_logit, preferred_element_type=jnp.float32)
    out_total, gate_total = (grad_out_w, grad_gate_w)
    grad_comb = jnp.dot(grad_mixed, w_out.T, preferred_element_type=jnp.float32).reshape(
        slots, row_part, tile_len, hidden_w
    )
    grad_pair = jnp.dot(grad_logit, w_gate.T, preferred_element_type=jnp.float32).reshape(
        slots, row_part, tile_len, channels
    )
    pair_back = norm_back(grad_pair, pair_hat, pair_inv, norm_gain).astype(jnp.bfloat16)
    comb_back = norm_back(grad_comb, comb_hat, comb_inv, out_gain).astype(jnp.bfloat16)
    left_term = rounded(
        jnp.einsum("sijh,kjh->ksih", comb_back, right_full, preferred_element_type=jnp.float32)
    )
    routed = jnp.einsum("ksih,sb->kbih", left_term, selector)
    column_sum = lax.psum_scatter(
        routed.astype(jnp.bfloat16), "col", scatter_dimension=1, tiled=True
    ).astype(jnp.float32)
    returned = lax.all_to_all(
        column_sum.reshape(row_count, k_local, row_part, hidden_w).astype(jnp.bfloat16),
        "row",
        split_axis=0,
        concat_axis=2,
        tiled=True,
    ).astype(jnp.float32)
    left_grad = returned.reshape(k_local, tile_len, hidden_w)
    right_part = jnp.einsum(
        "sijh,ksih->skjh", comb_back, chosen, preferred_element_type=jnp.float32
    )
    right_grad = jnp.sum(
        lax.psum_scatter(
            right_part.astype(jnp.bfloat16), "row", scatter_dimension=1, tiled=True
        ).astype(jnp.float32),
        axis=0,
    )
    grad_project = jnp.concatenate(
        [
            left_grad * left_sig,
            left_grad * left_proj * left_sig * (1.0 - left_sig),
            right_grad * right_sig,
            right_grad * right_proj * right_sig * (1.0 - right_sig),
        ],
        axis=-1,
    ).astype(jnp.bfloat16)
    flat_grad = grad_project.reshape(-1, 4 * hidden_w)
    grad_in_w = jnp.dot(flat_norm.T, flat_grad, preferred_element_type=jnp.float32)
    grad_norm = jnp.dot(flat_grad, w_in.T, preferred_element_type=jnp.float32).reshape(
        k_local, tile_len, channels
    )
    grad_slab = norm_back(grad_norm, slab_hat, slab_inv, norm_gain).astype(jnp.bfloat16)
    in_total, out_total, gate_total = lax.psum((grad_in_w, out_total, gate_total), ("col", "row"))
    update_out = update.reshape(1, slots, row_part, tile_len, channels)
    tiles_out = pair_back.reshape(1, slots, row_part, tile_len, channels)
    return (update_out, grad_slab, tiles_out, in_total, out_total, gate_total)


def solution(mesh):
    return jax.shard_map(
        body,
        mesh=mesh,
        in_specs=(
            P(("groups", "row"), "col", None),
            P(("groups", "col"), None, "row", None, None),
            P(("groups", "col"), None, "row", None, None),
            P(("groups", "col"), None),
            P(("groups", "col")),
            P(),
            P(),
            P(),
            P(),
            P(),
            P(),
            P(),
        ),
        out_specs=(
            P(("groups", "col"), None, "row", None, None),
            P(("groups", "row"), "col", None),
            P(("groups", "col"), None, "row", None, None),
            P("groups", None),
            P("groups", None),
            P("groups", None),
        ),
        check_vma=False,
    )
```

profile of v0, /device:TPU:0, one launch (start us, length us, event | category | flops | bytes accessed | tf_op | source)
XLA Modules:
  0.0 365.0 jit_solution(873537648331085904)
XLA Ops:
  14.5 4.2 %all-to-all-start = ((bf16[16,4,32,128]{3,2,0,1:T(8,128)(2,1)}), bf16[16,4,32,128]{3,2,0,1:T(8,128)(2,1)S(1)}, u32[]{:S(2)}, u32[]{:S(2)}) async-start(bf16[16,4,32,128]{3,2,0,1:T(8,128)(2,1)} %copy.57), calls=%async_computation | async-start | bytes 1048576 | tf_op jit(solution)/shard_map/all_to_all | solution.py:64
  19.5 9.8 %all-to-all-done = bf16[16,4,32,128]{3,2,0,1:T(8,128)(2,1)S(1)} async-done(((bf16[16,4,32,128]{3,2,0,1:T(8,128)(2,1)}), bf16[16,4,32,128]{3,2,0,1:T(8,128)(2,1)S(1)}, u32[]{:S(2)}, u32[]{:S(2)}) %all-to-all-start) | async-done | bytes 524320 | tf_op jit(solution)/shard_map/all_to_all | solution.py:64
  33.4 3.5 add_convert_fusion.1
  36.9 3.4 all-gather.3.cloned.1.call-done
  40.3 4.5 %copy.74 = bf16[4,16,128,128,1]{2,1,4,3,0:T(8,128)(2,1)} copy(bf16[4,16,128,128,1]{3,2,1,0,4:T(8,128)(2,1)} %bitcast.112) | data formatting | bytes 4194304 | tf_op jit(solution)/shard_map/reshape | solution.py:77
  44.8 4.2 %copy.75 = bf16[64,128,128,1]{1,0,3,2:T(8,128)(2,1)} copy(bf16[64,128,128,1]{2,1,0,3:T(8,128)(2,1)} %bitcast.113) | data formatting | bytes 4194304 | tf_op jit(solution)/shard_map/all_gather | solution.py:73
  49.0 40.4 %all-gather.5.cloned.1.call-done = bf16[64,4,32,128]{3,2,1,0:T(8,128)(2,1)} async-done(((bf16[64,1,32,128]{3,2,1,0:T(8,128)(2,1)}), bf16[64,4,32,128]{3,2,1,0:T(8,128)(2,1)}) %all-gather.5.cloned.1.call-update) | async-done | bytes 2097168 | tf_op jit(solution)/shard_map/all_gather | solution.py:71
  89.5 3.3 gather_fusion
  95.2 7.2 %copy.61 = bf16[4,16,2,32,128]{3,1,2,4,0:T(8,128)(2,1)} copy(bf16[4,16,2,32,128]{4,3,2,1,0:T(8,128)(2,1)} %broadcast_select_fusion.1) | data formatting | bytes 2097152 | tf_op jit(solution)/shard_map/jit(_take)/select_n | solution.py:72
  102.4 5.2 %convert_bitcast_fusion = bf16[4,2,32,128,128]{3,2,1,4,0:T(8,128)(2,1)S(1)} fusion(bf16[4,16,128,128,1]{2,1,4,3,0:T(8,128)(2,1)} %copy.74, bf16[4,16,2,32,128]{3,1,2,4,0:T(8,128)(2,1)} %copy.61), kind=kOutput, calls=%fused_computation.7 | convolution fusion | flops 138412032 | bytes 11534336 | tf_op jit(solution)/shard_map/gksih,gkjh->gsijh/dot_general | solution.py:74
  107.7 5.1 %convert_reduce_fusion = (f32[2,32,128]{2,1,0:T(8,128)S(1)}, f32[2,32,128,128]{2,1,0,3:T(8,128)}) fusion(bf16[4,2,32,128,128]{3,2,1,4,0:T(8,128)(2,1)S(1)} %convert_bitcast_fusion), kind=kLoop, calls=%fused_computation.1 | loop fusion | flops 11526144 | bytes 12615680 | tf_op jit(solution)/shard_map/reduce_sum | solution.py:10
  112.7 5.3 %copy.62 = f32[2,32,128,128]{3,2,1,0:T(8,128)} copy(f32[2,32,128,128]{2,1,0,3:T(8,128)} %get-tuple-element.31) | data formatting | bytes 8388608 | tf_op jit(solution)/shard_map/reduce_sum | solution.py:80
  118.1 2.8 multiply_reduce_fusion.2
  121.5 4.5 %add_convert_fusion = bf16[8192,128]{1,0:T(8,128)(2,1)S(1)} fusion(f32[2,32,128,128]{3,2,1,0:T(8,128)S(1)} %copy-done.2, f32[128]{0:T(128)S(1)} %copy-done.18, f32[128]{0:T(128)S(1)} %copy-done.15, f32[8192]{0:T(1024)S(1)} %bitcast.123, f32[8192]{0:T(1024)S(1)} %bitcast.119), kind=kLoop, calls=%fused_computation.28 | loop fusion | flops 5242880 | bytes 6358016 | tf_op jit(solution)/shard_map/convert_element_type | solution.py:82
  129.1 4.3 %fusion.8 = (bf16[8192,128]{1,0:T(8,128)(2,1)}, bf16[8192,128]{1,0:T(8,128)(2,1)}, bf16[8192,128]{1,0:T(8,128)(2,1)S(1)}) fusion(f32[8192,128]{1,0:T(8,128)S(1)} %fusion.48, bf16[1,2,32,128,128]{4,3,2,1,0:T(8,128)(2,1)S(1)} %copy-done.19, f32[8192]{0:T(1024)S(1)} %bitcast.132, bf16[8192,128]{1,0:T(8,128)(2,1)S(1)} %copy-done.7, ...), kind=kOutput, calls=%fused_computation.14 | convolution fusion | flops 284164096 | bytes 14745600 | tf_op jit(solution)/shard_map/dot_general | solution.py:88
  133.4 6.2 %multiply_reduce_fusion.4 = (f32[8192]{0:T(1024)S(1)}, f32[8192]{0:T(1024)S(1)}, f32[8192,128]{1,0:T(8,128)}) fusion(f32[128]{0:T(128)S(1)} %copy-done.15, f32[8192]{0:T(1024)S(1)} %bitcast.124, f32[8192]{0:T(1024)S(1)} %bitcast.120, f32[2,32,128,128]{3,2,1,0:T(8,128)S(1)} %copy-done.2, bf16[8192,128]{1,0:T(8,128)(2,1)S(1)} %get-tuple-element.43, ...), kind=kOutput, calls=%fused_computation.32 | convolution fusion | flops 274710528 | bytes 10650112 | tf_op jit(solution)/shard_map/dot_general | solution.py:97
  139.6 5.5 %copy.63 = f32[2,32,128,128]{2,1,0,3:T(8,128)} copy(f32[2,32,128,128]{3,2,1,0:T(8,128)} %bitcast.110) | data formatting | bytes 8388608 | tf_op jit(solution)/shard_map/reshape | solution.py:97
  145.1 4.8 %multiply_convert_fusion.1 = bf16[2,32,128,128]{2,1,0,3:T(8,128)(2,1)S(1)} fusion(f32[2,32,128,128]{2,1,0,3:T(8,128)} %copy.63, f32[2,32,128,128]{2,1,0,3:T(8,128)} %get-tuple-element.31, f32[2,32,128]{2,1,0:T(8,128)S(1)} %bitcast.128, f32[2,32,128]{2,1,0:T(8,128)S(1)} %bitcast.129, f32[128]{0:T(128)S(1)} %copy-done.15, f32[2,32,128]{2,1,0:T(8,128)S(1)} %add_rsqrt_fusion, ...), kind=kLoop, calls=%fused_computation.25 | loop fusion | flops 8388608 | bytes 10617344 | tf_op jit(solution)/shard_map/convert_element_type | solution.py:104
  151.3 2.5 convert_bitcast_fusion.3
  153.8 4.7 %copy.65 = bf16[64,2,32,128]{3,1,2,0:T(2,128)(2,1)} copy(bf16[64,2,32,128]{0,2,1,3:T(8,128)(2,1)} %convert_bitcast_fusion.3) | data formatting | bytes 2097152 | tf_op jit(solution)/shard_map/optimization_barrier | solution.py:24
  158.5 2.8 convert_bitcast_fusion.2
  165.4 5.4 %copy.68 = bf16[64,2,32,128]{0,2,3,1:T(8,128)(2,1)} copy(bf16[64,2,32,128]{3,2,0,1:T(8,128)(2,1)} %broadcast_select_fusion) | data formatting | bytes 2097152 | tf_op jit(solution)/shard_map/jit(_take)/select_n | solution.py:72
  170.8 5.5 %convert_bitcast_fusion.1 = bf16[2,64,128,128]{2,1,3,0:T(8,128)(2,1)} fusion(bf16[64,2,32,128]{0,2,3,1:T(8,128)(2,1)} %copy.68, bf16[2,32,128,128]{2,1,0,3:T(8,128)(2,1)} %copy-done.5), kind=kOutput, calls=%fused_computation.24 | convolution fusion | flops 136314880 | bytes 7340032 | tf_op jit(solution)/shard_map/sijh,ksih->skjh/dot_general | solution.py:120
  176.3 7.2 %multiply_reduce_fusion.3 = (f32[8192]{0:T(1024)S(1)}, f32[8192]{0:T(1024)S(1)}, f32[8192,128]{1,0:T(8,128)S(1)}) fusion(f32[128]{0:T(128)S(1)} %copy-done.16, f32[8192]{0:T(1024)S(1)} %bitcast.127, f32[8192]{0:T(1024)S(1)} %bitcast.122, bf16[1,2,32,128,128]{4,3,2,1,0:T(8,128)(2,1)S(1)} %copy-done.3, bf16[8192,128]{1,0:T(8,128)(2,1)} %get-tuple-element.41, ...), kind=kOutput, calls=%fused_computation.31 | convolution fusion | flops 275759104 | bytes 8552960 | tf_op jit(solution)/shard_map/dot_general | solution.py:100
  183.5 5.9 %multiply_convert_fusion = bf16[1,2,32,128,128]{4,3,2,1,0:T(8,128)(2,1)} fusion(f32[1,2,32,128,128]{4,3,2,1,0:T(8,128)S(1)} %bitcast.115, bf16[1,2,32,128,128]{4,3,2,1,0:T(8,128)(2,1)S(1)} %copy-done.3, f32[2,32,128]{2,1,0:T(8,128)S(1)} %bitcast.130, f32[2,32,128]{2,1,0:T(8,128)S(1)} %broadcast_multiply_fusion.5, f32[2,32,128]{2,1,0:T(8,128)S(1)} %bitcast.131, ...), kind=kLoop, calls=%fused_computation.22 | loop fusion | flops 9437184 | bytes 8520192 | tf_op jit(solution)/shard_map/convert_element_type | solution.py:103
  189.5 16.3 %reduce-scatter.3.cloned.1.call-done = bf16[64,1,32,128]{3,2,0,1:T(8,128)(2,1)} async-done(((bf16[64,4,32,128]{3,2,0,1:T(8,128)(2,1)}), bf16[64,1,32,128]{3,2,0,1:T(8,128)(2,1)}) %reduce-scatter.3.cloned.1.call-update) | async-done | bytes 524304 | tf_op jit(solution)/shard_map/reduce_scatter | solution.py:109
  205.8 3.5 all-to-all-start.1
  209.6 3.8 %fusion.49 = f32[128,128]{1,0:T(8,128)} fusion(bf16[8192,128]{1,0:T(8,128)(2,1)} %copy-done.4, bf16[8192,128]{1,0:T(8,128)(2,1)} %copy-done.9), kind=kOutput, calls=%fused_computation.105 | convolution fusion | flops 268435456 | bytes 4259840 | tf_op jit(solution)/shard_map/dot_general | solution.py:94
  214.7 3.4 all-to-all-done.1
  218.3 33.9 %reduce-scatter.5.cloned.1.call-done = bf16[2,16,128,128]{2,1,3,0:T(8,128)(2,1)} async-done(((bf16[2,64,128,128]{2,1,3,0:T(8,128)(2,1)}), bf16[2,16,128,128]{2,1,3,0:T(8,128)(2,1)}) %reduce-scatter.5.cloned.1.call-update) | async-done | bytes 1048592 | tf_op jit(solution)/shard_map/reduce_scatter | solution.py:124
  255.0 3.6 multiply_convert_fusion.6
  264.0 89.8 %all-reduce.3.cloned.1.call-done = (f32[128,512]{1,0:T(8,128)}, f32[128,128]{1,0:T(8,128)}, f32[128,128]{1,0:T(8,128)}) async-done(((f32[128,512]{1,0:T(8,128)}, f32[128,128]{1,0:T(8,128)}, f32[128,128]{1,0:T(8,128)}), (f32[128,512]{1,0:T(8,128)}, f32[128,128]{1,0:T(8,128)}, f32[128,128]{1,0:T(8,128)})) %all-reduce.3.cloned.1.call-update) | async-done | bytes 393232 | tf_op jit(solution)/shard_map/psum | solution.py:144
  (95 shorter events, 37.7 us)
Async XLA Ops:
  7.2 1.7 copy-start
  7.2 33.2 %all-gather.3.cloned.1.call-start = ((), (), s32[]{:S(2)}) async-start(), calls=%async_computation.4 | async-start | bytes 2621440 | tf_op jit(solution)/shard_map/all_gather | solution.py:73
  10.4 1.9 copy-start.1
  12.3 7.2 %copy-start.21 = (s32[1,2]{1,0:T(1,128)S(1)}, s32[1,2]{1,0:T(1,128)}, u32[]{:S(2)}) copy-start(s32[1,2]{1,0:T(1,128)} %param.15) | copy-start | bytes 28
  12.3 17.9 %copy-start.3 = (bf16[1,2,32,128,128]{4,3,2,1,0:T(8,128)(2,1)S(1)}, bf16[1,2,32,128,128]{4,3,2,1,0:T(8,128)(2,1)}, u32[]{:S(2)}) copy-start(bf16[1,2,32,128,128]{4,3,2,1,0:T(8,128)(2,1)} %param.13) | copy-start | bytes 6291460
  13.7 19.8 %copy-start.16 = (f32[128]{0:T(128)S(1)}, f32[128]{0:T(128)}, u32[]{:S(2)}) copy-start(f32[128]{0:T(128)} %param.17) | copy-start | bytes 1540
  13.7 19.8 %copy-start.17 = (f32[128]{0:T(128)S(1)}, f32[128]{0:T(128)}, u32[]{:S(2)}) copy-start(f32[128]{0:T(128)} %param.18) | copy-start | bytes 1540
  14.5 14.8 %all-to-all-start = ((bf16[16,4,32,128]{3,2,0,1:T(8,128)(2,1)}), bf16[16,4,32,128]{3,2,0,1:T(8,128)(2,1)S(1)}, u32[]{:S(2)}, u32[]{:S(2)}) async-start(bf16[16,4,32,128]{3,2,0,1:T(8,128)(2,1)} %copy.57), calls=%async_computation | async-start | bytes 1048576 | tf_op jit(solution)/shard_map/all_to_all | solution.py:64
  18.7 70.7 %all-gather.5.cloned.1.call-start = ((), (), s32[]{:S(2)}) async-start(), calls=%async_computation.5 | async-start | bytes 2621440 | tf_op jit(solution)/shard_map/all_gather | solution.py:71
  29.3 0.8 copy-start.11
  30.1 175.6 %reduce-scatter.3.cloned.1.call-start = ((), (), s32[]{:S(2)}) async-start(), calls=%async_computation.6 | async-start | bytes 2621440 | tf_op jit(solution)/shard_map/reduce_scatter | solution.py:109
  118.1 3.4 copy-start.2
  118.1 3.4 copy-start.15
  118.1 3.5 copy-start.18
  120.9 5.2 %copy-start.14 = (bf16[128,128]{1,0:T(8,128)(2,1)S(1)}, bf16[128,128]{1,0:T(8,128)(2,1)}, u32[]{:S(2)}) copy-start(bf16[128,128]{1,0:T(8,128)(2,1)} %param.22) | copy-start | bytes 98308
  126.1 1.3 copy-start.4
  126.1 2.3 copy-start.7
  126.1 3.0 copy-start.19
  126.1 3.0 copy-start.20
  133.4 6.2 %copy-start.9 = (bf16[8192,128]{1,0:T(8,128)(2,1)}, bf16[8192,128]{1,0:T(8,128)(2,1)S(1)}, u32[]{:S(2)}) copy-start(bf16[8192,128]{1,0:T(8,128)(2,1)S(1)} %get-tuple-element.43) | copy-start | bytes 6291460
  145.1 6.2 %copy-start.6 = (bf16[64,128,128,1]{1,0,3,2:T(8,128)(2,1)S(1)}, bf16[64,128,128,1]{1,0,3,2:T(8,128)(2,1)}, u32[]{:S(2)}) copy-start(bf16[64,128,128,1]{1,0,3,2:T(8,128)(2,1)} %copy.75) | copy-start | bytes 6291460
  149.9 1.4 copy-start.5
  163.0 89.1 %reduce-scatter.5.cloned.1.call-start = ((), (), s32[]{:S(2)}) async-start(), calls=%async_computation.7 | async-start | bytes 5242880 | tf_op jit(solution)/shard_map/reduce_scatter | solution.py:124
  189.5 23.9 %copy-start.8 = (bf16[8192,128]{1,0:T(8,128)(2,1)S(1)}, bf16[8192,128]{1,0:T(8,128)(2,1)}, u32[]{:S(2)}) copy-start(bf16[8192,128]{1,0:T(8,128)(2,1)} %add_convert_fusion.1) | copy-start | bytes 6291460
  205.8 12.3 %all-to-all-start.1 = ((bf16[4,16,32,128]{3,2,1,0:T(8,128)(2,1)}), bf16[4,16,32,128]{3,2,1,0:T(8,128)(2,1)S(1)}, u32[]{:S(2)}, u32[]{:S(2)}) async-start(bf16[4,16,32,128]{3,2,1,0:T(8,128)(2,1)} %bitcast.125), calls=%async_computation.2 | async-start | bytes 1048576 | tf_op jit(solution)/shard_map/all_to_all | solution.py:112
  209.2 144.6 %all-reduce.3.cloned.1.call-start = ((), (), s32[]{:S(2)}) async-start(), calls=%async_computation.8 | async-start | bytes 786432 | tf_op jit(solution)/shard_map/psum | solution.py:144
  209.5 3.8 %copy-start.10 = (bf16[8192,128]{1,0:T(8,128)(2,1)S(1)}, bf16[8192,128]{1,0:T(8,128)(2,1)}, u32[]{:S(2)}) copy-start(bf16[8192,128]{1,0:T(8,128)(2,1)} %get-tuple-element.41) | copy-start | bytes 6291460
  258.6 0.8 copy-start.13
  258.7 2.0 copy-start.12
Sparse Core Ops, SparseCore 0:
  13.8 26.4 all-gather.2
  42.5 46.9 all-gather.4
  163.1 42.5 reduce-scatter.2
  208.3 43.8 reduce-scatter.4
  262.8 90.9 all-reduce.2
where the time goes:
time: 366 us; the launch traced here: 365 us
  waiting for transfers between devices  197 us (54%)
  local copies, waits for them, and re-layouts  60.2 us (16%)
  matrix products  44.3 us (12%)
  other arithmetic  40.4 us (11%)
  between operations  14.8 us (4%)
  starting transfers between devices  8.1 us (2%)
    psum x1, waiting for transfers between devices, body(): lax.psum((grad_in_w, out_total, gate_total), ('col', 'row'))  89.8 us
    all_gather x1, waiting for transfers between devices, body(): panels = lax.all_gather(spread, 'col', axis=1, tiled=True)  40.4 us
    reduce_scatter x1, waiting for transfers between devices, body(): lax.psum_scatter(right_part.astype(jnp.bfloat16), 'row', scatter_dimensio...  33.9 us
    reduce_scatter x1, waiting for transfers between devices, body(): lax.psum_scatter(routed.astype(jnp.bfloat16), 'col', scatter_dimension=1,...  16.3 us
    unnamed x51, local copies, waits for them, and re-layouts  14.8 us
    select_n x2, local copies, waits for them, and re-layouts, body(): chosen = jnp.take(panels, row_blocks, axis=1)  12.6 us
    all_to_all x1, waiting for transfers between devices, body(): lax.all_to_all(left_edges.reshape(k_local, row_count, row_part, hidden_w)...  9.82 us
  transfers between devices with their start and end apart: 7, of which 7 were waited for; matrix products, arithmetic and copies ran while one was open for 14% of the time, Pallas kernels for 0%

commit v1 on v0

--- a/solution.py
+++ b/solution.py
@@ -61,13 +61,19 @@
     selector = (row_blocks[:, None] == jnp.arange(col_count)[None, :]).astype(jnp.float32) * active[
         :, None
     ]
-    spread = lax.all_to_all(
-        left_edges.reshape(k_local, row_count, row_part, hidden_w),
-        "row",
-        split_axis=1,
-        concat_axis=0,
-        tiled=True,
-    )
+    shard = left_edges.reshape(k_local, row_count, row_part, hidden_w)
+    ways, here = (lax.axis_size("row"), lax.axis_index("row"))
+    width = shard.shape[1] // ways
+    shape = list(shard.shape)
+    shape[1] = width
+    height = shape[0]
+    shape[0] = height * ways
+    spread = jnp.zeros(shape, shard.dtype)
+    for mask in range(ways):
+        part = lax.dynamic_slice_in_dim(shard, (here ^ mask) * width, width, axis=1)
+        if mask:
+            part = lax.ppermute(part, "row", [(d, d ^ mask) for d in range(ways)])
+        spread = lax.dynamic_update_slice_in_dim(spread, part, (here ^ mask) * height, axis=0)
     panels = lax.all_gather(spread, "col", axis=1, tiled=True)
     chosen = jnp.take(panels, row_blocks, axis=1)
     right_full = lax.all_gather(right_edges, "row", axis=0, tiled=True)

time: 366 us -> 364 us (level)
  waiting for transfers between devices: 197 us -> 192 us
    all_to_all x1 -> x0, waiting for transfers between devices: 9.82 us -> none  [body(): lax.all_to_all(left_edges.reshape(k_local, row_count, row_part, hidden_w)...]
    all_to_all x1 -> x0, starting transfers between devices: 4.21 us -> none  [body(): lax.all_to_all(left_edges.reshape(k_local, row_count, row_part, hidden_w)...]
    ppermute x0 -> x3, waiting for transfers between devices: none -> 3.9 us  [body(): part = lax.ppermute(part, 'row', [(d, d ^ mask) for d in range(ways)])]
  transfers between devices with their start and end apart: 7 -> 9, of which waited for: 7 -> 8; matrix products, arithmetic and copies ran while one was open for 14% -> 15% of each run, Pallas kernels for 0% -> 0%
where the time goes in v1:
time: 364 us; the launch traced here: 363 us
  waiting for transfers between devices  192 us (53%)
  local copies, waits for them, and re-layouts  62.8 us (17%)
  matrix products  44.3 us (12%)
  other arithmetic  42.4 us (12%)
  between operations  14.8 us (4%)
  starting transfers between devices  7.02 us (2%)
    psum x1, waiting for transfers between devices, body(): lax.psum((grad_in_w, out_total, gate_total), ('col', 'row'))  89.8 us
    all_gather x1, waiting for transfers between devices, body(): panels = lax.all_gather(spread, 'col', axis=1, tiled=True)  39.8 us
    reduce_scatter x1, waiting for transfers between devices, body(): lax.psum_scatter(right_part.astype(jnp.bfloat16), 'row', scatter_dimensio...  33.9 us
    reduce_scatter x1, waiting for transfers between devices, body(): lax.psum_scatter(routed.astype(jnp.bfloat16), 'col', scatter_dimension=1,...  15.6 us
    unnamed x51, local copies, waits for them, and re-layouts  15.4 us
    select_n x2, local copies, waits for them, and re-layouts, body(): chosen = jnp.take(panels, row_blocks, axis=1)  12.6 us
  transfers between devices with their start and end apart: 9, of which 8 were waited for; matrix products, arithmetic and copies ran while one was open for 15% of the time, Pallas kernels for 0%

profile of v1, /device:TPU:0, one launch (start us, length us, event | category | flops | bytes accessed | tf_op | source)
XLA Modules:
  0.0 363.2 jit_solution(826310761054450333)
XLA Ops:
  15.8 2.5 collective-permute-start.1
  27.1 2.5 fusion.11
  29.7 4.1 %add_convert_fusion.1 = bf16[8192,128]{1,0:T(8,128)(2,1)} fusion(bf16[1,2,32,128,128]{4,3,2,1,0:T(8,128)(2,1)S(1)} %copy-done.3, f32[128]{0:T(128)} %param.18, f32[128]{0:T(128)} %param.17, f32[8192]{0:T(1024)S(1)} %bitcast.118, f32[8192]{0:T(1024)S(1)} %bitcast.113), kind=kLoop, calls=%fused_computation.30 | loop fusion | flops 6291456 | bytes 4260864 | tf_op jit(solution)/shard_map/convert_element_type | solution.py:90
  33.8 5.3 %all-gather.3.cloned.1.call-done = bf16[64,128,128]{2,1,0:T(8,128)(2,1)} async-done(((bf16[16,128,128]{2,1,0:T(8,128)(2,1)}), bf16[64,128,128]{2,1,0:T(8,128)(2,1)}) %all-gather.3.cloned.1.call-update) | async-done | bytes 2097168 | tf_op jit(solution)/shard_map/all_gather | solution.py:79
  39.1 4.5 %copy.68 = bf16[4,16,128,128,1]{2,1,4,3,0:T(8,128)(2,1)} copy(bf16[4,16,128,128,1]{3,2,1,0,4:T(8,128)(2,1)} %bitcast.105) | data formatting | bytes 4194304 | tf_op jit(solution)/shard_map/reshape | solution.py:83
  43.6 4.2 %copy.69 = bf16[64,128,128,1]{1,0,3,2:T(8,128)(2,1)} copy(bf16[64,128,128,1]{2,1,0,3:T(8,128)(2,1)} %bitcast.106) | data formatting | bytes 4194304 | tf_op jit(solution)/shard_map/all_gather | solution.py:79
  47.8 39.8 %all-gather.5.cloned.1.call-done = bf16[64,4,32,128]{3,2,1,0:T(8,128)(2,1)} async-done(((bf16[64,1,32,128]{3,2,1,0:T(8,128)(2,1)}), bf16[64,4,32,128]{3,2,1,0:T(8,128)(2,1)}) %all-gather.5.cloned.1.call-update) | async-done | bytes 2097168 | tf_op jit(solution)/shard_map/all_gather | solution.py:77
  87.6 3.3 gather_fusion
  93.4 7.2 %copy.55 = bf16[4,16,2,32,128]{3,1,2,4,0:T(8,128)(2,1)} copy(bf16[4,16,2,32,128]{4,3,2,1,0:T(8,128)(2,1)} %broadcast_select_fusion.1) | data formatting | bytes 2097152 | tf_op jit(solution)/shard_map/jit(_take)/select_n | solution.py:78
  100.6 5.2 %convert_bitcast_fusion = bf16[4,2,32,128,128]{3,2,1,4,0:T(8,128)(2,1)S(1)} fusion(bf16[4,16,128,128,1]{2,1,4,3,0:T(8,128)(2,1)} %copy.68, bf16[4,16,2,32,128]{3,1,2,4,0:T(8,128)(2,1)} %copy.55), kind=kOutput, calls=%fused_computation.7 | convolution fusion | flops 138412032 | bytes 11534336 | tf_op jit(solution)/shard_map/gksih,gkjh->gsijh/dot_general | solution.py:80
  105.9 5.1 %convert_reduce_fusion = (f32[2,32,128]{2,1,0:T(8,128)S(1)}, f32[2,32,128,128]{2,1,0,3:T(8,128)}) fusion(bf16[4,2,32,128,128]{3,2,1,4,0:T(8,128)(2,1)S(1)} %convert_bitcast_fusion), kind=kLoop, calls=%fused_computation.1 | loop fusion | flops 11526144 | bytes 12615680 | tf_op jit(solution)/shard_map/reduce_sum | solution.py:10
  110.9 5.4 %copy.56 = f32[2,32,128,128]{3,2,1,0:T(8,128)} copy(f32[2,32,128,128]{2,1,0,3:T(8,128)} %get-tuple-element.31) | data formatting | bytes 8388608 | tf_op jit(solution)/shard_map/reduce_sum | solution.py:86
  116.3 2.8 multiply_reduce_fusion.2
  119.8 4.5 %add_convert_fusion = bf16[8192,128]{1,0:T(8,128)(2,1)S(1)} fusion(f32[2,32,128,128]{3,2,1,0:T(8,128)S(1)} %copy-done.2, f32[128]{0:T(128)S(1)} %copy-done.18, f32[128]{0:T(128)S(1)} %copy-done.15, f32[8192]{0:T(1024)S(1)} %bitcast.115, f32[8192]{0:T(1024)S(1)} %bitcast.111), kind=kLoop, calls=%fused_computation.28 | loop fusion | flops 5242880 | bytes 6358016 | tf_op jit(solution)/shard_map/convert_element_type | solution.py:88
  127.3 4.3 %fusion.8 = (bf16[8192,128]{1,0:T(8,128)(2,1)}, bf16[8192,128]{1,0:T(8,128)(2,1)}, bf16[8192,128]{1,0:T(8,128)(2,1)S(1)}) fusion(f32[8192,128]{1,0:T(8,128)S(1)} %fusion.48, bf16[1,2,32,128,128]{4,3,2,1,0:T(8,128)(2,1)S(1)} %copy-done.19, f32[8192]{0:T(1024)S(1)} %bitcast.124, bf16[8192,128]{1,0:T(8,128)(2,1)S(1)} %copy-done.7, ...), kind=kOutput, calls=%fused_computation.14 | convolution fusion | flops 284164096 | bytes 14745600 | tf_op jit(solution)/shard_map/dot_general | solution.py:94
  131.6 6.2 %multiply_reduce_fusion.4 = (f32[8192]{0:T(1024)S(1)}, f32[8192]{0:T(1024)S(1)}, f32[8192,128]{1,0:T(8,128)}) fusion(f32[128]{0:T(128)S(1)} %copy-done.15, f32[8192]{0:T(1024)S(1)} %bitcast.116, f32[8192]{0:T(1024)S(1)} %bitcast.112, f32[2,32,128,128]{3,2,1,0:T(8,128)S(1)} %copy-done.2, bf16[8192,128]{1,0:T(8,128)(2,1)S(1)} %get-tuple-element.43, ...), kind=kOutput, calls=%fused_computation.32 | convolution fusion | flops 274710528 | bytes 10650112 | tf_op jit(solution)/shard_map/dot_general | solution.py:103
  137.8 5.5 %copy.57 = f32[2,32,128,128]{2,1,0,3:T(8,128)} copy(f32[2,32,128,128]{3,2,1,0:T(8,128)} %bitcast.103) | data formatting | bytes 8388608 | tf_op jit(solution)/shard_map/reshape | solution.py:103
  143.3 4.8 %multiply_convert_fusion.1 = bf16[2,32,128,128]{2,1,0,3:T(8,128)(2,1)S(1)} fusion(f32[2,32,128,128]{2,1,0,3:T(8,128)} %copy.57, f32[2,32,128,128]{2,1,0,3:T(8,128)} %get-tuple-element.31, f32[2,32,128]{2,1,0:T(8,128)S(1)} %bitcast.120, f32[2,32,128]{2,1,0:T(8,128)S(1)} %bitcast.121, f32[128]{0:T(128)S(1)} %copy-done.15, f32[2,32,128]{2,1,0:T(8,128)S(1)} %add_rsqrt_fusion, ...), kind=kLoop, calls=%fused_computation.25 | loop fusion | flops 8388608 | bytes 10617344 | tf_op jit(solution)/shard_map/convert_element_type | solution.py:110
  149.5 2.5 convert_bitcast_fusion.3
  152.0 4.7 %copy.59 = bf16[64,2,32,128]{3,1,2,0:T(2,128)(2,1)} copy(bf16[64,2,32,128]{0,2,1,3:T(8,128)(2,1)} %convert_bitcast_fusion.3) | data formatting | bytes 2097152 | tf_op jit(solution)/shard_map/optimization_barrier | solution.py:24
  156.7 2.8 convert_bitcast_fusion.2
  163.6 5.4 %copy.62 = bf16[64,2,32,128]{0,2,3,1:T(8,128)(2,1)} copy(bf16[64,2,32,128]{3,2,0,1:T(8,128)(2,1)} %broadcast_select_fusion) | data formatting | bytes 2097152 | tf_op jit(solution)/shard_map/jit(_take)/select_n | solution.py:78
  169.0 5.5 %convert_bitcast_fusion.1 = bf16[2,64,128,128]{2,1,3,0:T(8,128)(2,1)} fusion(bf16[64,2,32,128]{0,2,3,1:T(8,128)(2,1)} %copy.62, bf16[2,32,128,128]{2,1,0,3:T(8,128)(2,1)} %copy-done.5), kind=kOutput, calls=%fused_computation.24 | convolution fusion | flops 136314880 | bytes 7340032 | tf_op jit(solution)/shard_map/sijh,ksih->skjh/dot_general | solution.py:126
  175.2 7.2 %multiply_reduce_fusion.3 = (f32[8192]{0:T(1024)S(1)}, f32[8192]{0:T(1024)S(1)}, f32[8192,128]{1,0:T(8,128)S(1)}) fusion(f32[128]{0:T(128)S(1)} %copy-done.16, f32[8192]{0:T(1024)S(1)} %bitcast.119, f32[8192]{0:T(1024)S(1)} %bitcast.114, bf16[1,2,32,128,128]{4,3,2,1,0:T(8,128)(2,1)S(1)} %copy-done.3, bf16[8192,128]{1,0:T(8,128)(2,1)} %get-tuple-element.41, ...), kind=kOutput, calls=%fused_computation.31 | convolution fusion | flops 275759104 | bytes 8552960 | tf_op jit(solution)/shard_map/dot_general | solution.py:106
  182.4 5.9 %multiply_convert_fusion = bf16[1,2,32,128,128]{4,3,2,1,0:T(8,128)(2,1)} fusion(f32[1,2,32,128,128]{4,3,2,1,0:T(8,128)S(1)} %bitcast.108, bf16[1,2,32,128,128]{4,3,2,1,0:T(8,128)(2,1)S(1)} %copy-done.3, f32[2,32,128]{2,1,0:T(8,128)S(1)} %bitcast.122, f32[2,32,128]{2,1,0:T(8,128)S(1)} %broadcast_multiply_fusion.5, f32[2,32,128]{2,1,0:T(8,128)S(1)} %bitcast.123, ...), kind=kLoop, calls=%fused_computation.22 | loop fusion | flops 9437184 | bytes 8520192 | tf_op jit(solution)/shard_map/convert_element_type | solution.py:109
  188.3 15.6 %reduce-scatter.3.cloned.1.call-done = bf16[64,1,32,128]{3,2,0,1:T(8,128)(2,1)} async-done(((bf16[64,4,32,128]{3,2,0,1:T(8,128)(2,1)}), bf16[64,1,32,128]{3,2,0,1:T(8,128)(2,1)}) %reduce-scatter.3.cloned.1.call-update) | async-done | bytes 524304 | tf_op jit(solution)/shard_map/reduce_scatter | solution.py:115
  203.9 3.5 all-to-all-start
  207.7 3.8 %fusion.49 = f32[128,128]{1,0:T(8,128)} fusion(bf16[8192,128]{1,0:T(8,128)(2,1)} %copy-done.4, bf16[8192,128]{1,0:T(8,128)(2,1)} %copy-done.9), kind=kOutput, calls=%fused_computation.112 | convolution fusion | flops 268435456 | bytes 4259840 | tf_op jit(solution)/shard_map/dot_general | solution.py:100
  212.9 3.3 all-to-all-done
  216.4 33.9 %reduce-scatter.5.cloned.1.call-done = bf16[2,16,128,128]{2,1,3,0:T(8,128)(2,1)} async-done(((bf16[2,64,128,128]{2,1,3,0:T(8,128)(2,1)}), bf16[2,16,128,128]{2,1,3,0:T(8,128)(2,1)}) %reduce-scatter.5.cloned.1.call-update) | async-done | bytes 1048592 | tf_op jit(solution)/shard_map/reduce_scatter | solution.py:130
  253.2 3.6 multiply_convert_fusion.6
  262.3 89.8 %all-reduce.3.cloned.1.call-done = (f32[128,512]{1,0:T(8,128)}, f32[128,128]{1,0:T(8,128)}, f32[128,128]{1,0:T(8,128)}) async-done(((f32[128,512]{1,0:T(8,128)}, f32[128,128]{1,0:T(8,128)}, f32[128,128]{1,0:T(8,128)}), (f32[128,512]{1,0:T(8,128)}, f32[128,128]{1,0:T(8,128)}, f32[128,128]{1,0:T(8,128)})) %all-reduce.3.cloned.1.call-update) | async-done | bytes 393232 | tf_op jit(solution)/shard_map/psum | solution.py:150
  (103 shorter events, 43.6 us)
Async XLA Ops:
  7.2 1.7 copy-start
  7.2 31.9 %all-gather.3.cloned.1.call-start = ((), (), s32[]{:S(2)}) async-start(), calls=%async_computation.3 | async-start | bytes 2621440 | tf_op jit(solution)/shard_map/all_gather | solution.py:79
  10.4 1.9 copy-start.1
  12.3 13.5 %copy-start.3 = (bf16[1,2,32,128,128]{4,3,2,1,0:T(8,128)(2,1)S(1)}, bf16[1,2,32,128,128]{4,3,2,1,0:T(8,128)(2,1)}, u32[]{:S(2)}) copy-start(bf16[1,2,32,128,128]{4,3,2,1,0:T(8,128)(2,1)} %param.13) | copy-start | bytes 6291460
  13.7 73.9 %all-gather.5.cloned.1.call-start = ((), (), s32[]{:S(2)}) async-start(), calls=%async_computation.4 | async-start | bytes 2621440 | tf_op jit(solution)/shard_map/all_gather | solution.py:77
  14.5 0.8 copy-start.11
  15.3 4.5 %collective-permute-start = (bf16[16,1,32,128]{3,2,1,0:T(8,128)(2,1)}, bf16[16,1,32,128]{3,2,1,0:T(8,128)(2,1)S(1)}, u32[]{:S(2)}, u32[]{:S(2)}) collective-permute-start(bf16[16,1,32,128]{3,2,1,0:T(8,128)(2,1)} %get-tuple-element.54), channel_id=1, source_target_pairs={{0,1},{1,0},{2,3},{3,2},{4,5},{5,4},{6,7},{7,6},{8,9},{9,8},{10,11... | collective-permute-start | bytes 393224 | tf_op jit(solution)/shard_map/ppermute | solution.py:75
  15.8 6.8 %collective-permute-start.1 = (bf16[16,1,32,128]{3,2,1,0:T(8,128)(2,1)S(1)}, bf16[16,1,32,128]{3,2,1,0:T(8,128)(2,1)S(1)}, u32[]{:S(2)}, u32[]{:S(2)}) collective-permute-start(bf16[16,1,32,128]{3,2,1,0:T(8,128)(2,1)S(1)} %get-tuple-element.53), channel_id=1, source_target_pairs={{0,2},{1,3},{2,0},{3,1},{4,6},{5,7},{6,4},{7,5},{8,10},{9,11},{10,... | collective-permute-start | bytes 393224 | tf_op jit(solution)/shard_map/ppermute | solution.py:75
  18.3 6.8 %collective-permute-start.2 = (bf16[16,1,32,128]{3,2,1,0:T(8,128)(2,1)S(1)}, bf16[16,1,32,128]{3,2,1,0:T(8,128)(2,1)S(1)}, u32[]{:S(2)}, u32[]{:S(2)}) collective-permute-start(bf16[16,1,32,128]{3,2,1,0:T(8,128)(2,1)S(1)} %get-tuple-element.52), channel_id=1, source_target_pairs={{0,3},{1,2},{2,1},{3,0},{4,7},{5,6},{6,5},{7,4},{8,11},{9,10},{10,... | collective-permute-start | bytes 393224 | tf_op jit(solution)/shard_map/ppermute | solution.py:75
  25.8 178.2 %reduce-scatter.3.cloned.1.call-start = ((), (), s32[]{:S(2)}) async-start(), calls=%async_computation.5 | async-start | bytes 2621440 | tf_op jit(solution)/shard_map/reduce_scatter | solution.py:115
  116.3 3.4 copy-start.2
  116.3 3.4 copy-start.15
  116.3 3.5 copy-start.18
  119.1 5.2 %copy-start.14 = (bf16[128,128]{1,0:T(8,128)(2,1)S(1)}, bf16[128,128]{1,0:T(8,128)(2,1)}, u32[]{:S(2)}) copy-start(bf16[128,128]{1,0:T(8,128)(2,1)} %param.22) | copy-start | bytes 98308
  124.3 1.3 copy-start.4
  124.3 2.3 copy-start.7
  124.3 3.0 copy-start.19
  124.3 3.0 copy-start.20
  131.6 6.2 %copy-start.9 = (bf16[8192,128]{1,0:T(8,128)(2,1)}, bf16[8192,128]{1,0:T(8,128)(2,1)S(1)}, u32[]{:S(2)}) copy-start(bf16[8192,128]{1,0:T(8,128)(2,1)S(1)} %get-tuple-element.43) | copy-start | bytes 6291460
  143.3 6.1 %copy-start.6 = (bf16[64,128,128,1]{1,0,3,2:T(8,128)(2,1)S(1)}, bf16[64,128,128,1]{1,0,3,2:T(8,128)(2,1)}, u32[]{:S(2)}) copy-start(bf16[64,128,128,1]{1,0,3,2:T(8,128)(2,1)} %copy.69) | copy-start | bytes 6291460
  148.1 1.4 copy-start.5
  149.4 7.2 %copy-start.21 = (s32[1,2]{1,0:T(1,128)S(1)}, s32[1,2]{1,0:T(1,128)}, u32[]{:S(2)}) copy-start(s32[1,2]{1,0:T(1,128)} %param.15) | copy-start | bytes 28
  161.2 89.1 %reduce-scatter.5.cloned.1.call-start = ((), (), s32[]{:S(2)}) async-start(), calls=%async_computation.6 | async-start | bytes 5242880 | tf_op jit(solution)/shard_map/reduce_scatter | solution.py:130
  174.5 0.7 copy-start.16
  188.3 23.2 %copy-start.8 = (bf16[8192,128]{1,0:T(8,128)(2,1)S(1)}, bf16[8192,128]{1,0:T(8,128)(2,1)}, u32[]{:S(2)}) copy-start(bf16[8192,128]{1,0:T(8,128)(2,1)} %add_convert_fusion.1) | copy-start | bytes 6291460
  203.9 12.3 %all-to-all-start = ((bf16[4,16,32,128]{3,2,1,0:T(8,128)(2,1)}), bf16[4,16,32,128]{3,2,1,0:T(8,128)(2,1)S(1)}, u32[]{:S(2)}, u32[]{:S(2)}) async-start(bf16[4,16,32,128]{3,2,1,0:T(8,128)(2,1)} %bitcast.117), calls=%async_computation.1 | async-start | bytes 1048576 | tf_op jit(solution)/shard_map/all_to_all | solution.py:118
  207.4 144.7 %all-reduce.3.cloned.1.call-start = ((), (), s32[]{:S(2)}) async-start(), calls=%async_computation.7 | async-start | bytes 786432 | tf_op jit(solution)/shard_map/psum | solution.py:150
  207.7 3.8 %copy-start.10 = (bf16[8192,128]{1,0:T(8,128)(2,1)S(1)}, bf16[8192,128]{1,0:T(8,128)(2,1)}, u32[]{:S(2)}) copy-start(bf16[8192,128]{1,0:T(8,128)(2,1)} %get-tuple-element.41) | copy-start | bytes 6291460
  253.2 4.4 %copy-start.17 = (f32[128]{0:T(128)S(1)}, f32[128]{0:T(128)}, u32[]{:S(2)}) copy-start(f32[128]{0:T(128)} %param.18) | copy-start | bytes 1540
  256.9 0.8 copy-start.13
  256.9 2.0 copy-start.12
Sparse Core Ops, SparseCore 0:
  13.8 25.2 all-gather.2
  41.3 46.3 all-gather.4
  161.3 42.5 reduce-scatter.2
  206.5 43.8 reduce-scatter.4
  261.1 90.9 all-reduce.2
